TPU v7x, 32 devices: a whole 2x2x4 slice. The times are simulated.
32 devices in a mesh: ctx: 8 (over z, x), head: 4 (over y, core).
Axes of the slice: x: 2, y: 2, z: 4, core: 2. Of those that a mesh axis runs over, the one named last changes fastest.
Arguments:
- queries: bfloat16 [8192, 2048], P('ctx', 'head'), may hold values from -8 to 8
- keys: bfloat16 [8192, 2048], P('ctx', 'head'), may hold values from -8 to 8
- values: bfloat16 [8192, 2048], P('ctx', 'head'), may hold values from -6 to 6
- out_weight: bfloat16 [4096, 2048], P(None, 'head'), may hold values from -0.125 to 0.125
- out_grad: bfloat16 [8192, 4096], P('ctx', 'head'), may hold values from -6 to 6
- long_blocks: int32 [16, 4], replicated, may hold values from 0 to 15, as said below
Outputs:
- layer_out: bfloat16 [8192, 4096], P('ctx', 'head')
- query_grad: bfloat16 [8192, 2048], P('ctx', 'head')
- key_grad: bfloat16 [8192, 2048], P('ctx', 'head')
- value_grad: bfloat16 [8192, 2048], P('ctx', 'head')
Inputs may be any that keep to these rules, and one draw needn't show every extreme that they name: `long_blocks`: row b names 4 different blocks. The 8 blocks named by the rows of the 2 query blocks held by one index of ctx lie on 8 different indices of ctx. A row may name its own block.
All inputs are finite; a program needn't handle non-finite values.
Results may differ from a plain program's by a relative error of at most 0.019.
Values may be sent and summed in bfloat16 or wider, within the bound.
A program may use at most 192 MiB of HBM per device.

v0:
```python
import functools
import math

import jax
import jax.numpy as jnp
from jax import lax
from jax.experimental import pallas as pl
from jax.experimental.pallas import tpu as pltpu
from jax.sharding import PartitionSpec as P

HD = 128
LIN_DEV = 3
LISTED = 4
BLOCK = 512
CHUNK = 256
SCALING = 1.0 / math.sqrt(HD)
MESH = pl.DeviceIdType.MESH
VMEM_LIMIT = 56 * 1024 * 1024


def mm(a, b):
    return jnp.dot(a, b, preferred_element_type=jnp.float32)


def mm_nt(a, b):
    return lax.dot_general(a, b, (((1,), (1,)), ((), ())), preferred_element_type=jnp.float32)


def mm_tn(a, b):
    return lax.dot_general(a, b, (((0,), (0,)), ((), ())), preferred_element_type=jnp.float32)


def bf16(x):
    return x.astype(jnp.bfloat16)


def block_scale(ctx_place, row_count, b):
    first = ctx_place * row_count + b * BLOCK
    rows = lax.broadcasted_iota(jnp.int32, (BLOCK, HD), 0) + (first + 1)
    scale = 1.0 / (math.sqrt(HD) * jnp.sqrt(rows.astype(jnp.float32)))
    return scale


def causal_mask():
    u = lax.broadcasted_iota(jnp.int32, (BLOCK, BLOCK), 0)
    s = lax.broadcasted_iota(jnp.int32, (BLOCK, BLOCK), 1)
    return u >= s


def remote(src, dst, send, recv, target):
    return pltpu.make_async_remote_copy(
        src_ref=src, dst_ref=dst, send_sem=send, recv_sem=recv, device_id=target, device_id_type=MESH
    )


def enter(n_ctx, me, sib, par):
    barrier = pltpu.get_barrier_semaphore()
    for other in (sib, par):
        pl.semaphore_signal(barrier, inc=1, device_id={"head": other}, device_id_type=MESH)

    def greet(s, carry):
        to = lax.rem(me + s, n_ctx)
        pl.semaphore_signal(barrier, inc=1, device_id={"ctx": to}, device_id_type=MESH)
        return carry

    lax.fori_loop(1, n_ctx, greet, 0)
    pl.semaphore_wait(barrier, n_ctx + 1)


def gather_kernel(
    n_ctx, within, q, k, v, og, w,
    g_out, lin_out, state_out, kv_in,
    og_sib, og_par, og_far, kv_out, st_blk, st_out, st_in, total,
    sib_sems, par_send, par_recv, far_send, far_recv, kv_send, kv_recv, st_send, st_recv, own_sem,
):
    me = lax.axis_index("ctx")
    h = lax.axis_index("head")
    sib = h + 1 - 2 * lax.rem(h, 2)
    par = lax.rem(h + 2, 4)
    far = lax.rem(sib + 2, 4)
    rows, width = og.shape
    nblocks = rows // BLOCK
    chunks = rows // CHUNK
    enter(n_ctx, me, sib, par)

    def part(c):
        return pl.ds(pl.multiple_of(c * CHUNK, CHUNK), CHUNK)

    def par_copy(c):
        return remote(og.at[part(c)], og_par.at[part(c)], par_send.at[c], par_recv.at[c], {"head": par})

    def far_copy(c):
        return remote(og_par.at[part(c)], og_far.at[part(c)], far_send.at[c], far_recv.at[c], {"head": sib})

    sib_copy = remote(og, og_sib, sib_sems.at[0], sib_sems.at[1], {"head": sib})

    def kv_copy(s):
        to = lax.rem(me + s, n_ctx)
        return remote(kv_out.at[s], kv_in.at[me], kv_send.at[s], kv_recv.at[s], {"ctx": to})

    def st_copy(s):
        to = lax.rem(me + s, n_ctx)
        return remote(st_out, st_in.at[me], st_send.at[s], st_recv.at[s], {"ctx": to})

    def loop(first, last, step):
        def body(i, carry):
            step(i)
            return carry

        lax.fori_loop(first, last, body, 0)

    loop(0, chunks, lambda c: par_copy(c).start())

    def fill(s):
        to = lax.rem(me + s, n_ctx)
        picked_k = jnp.zeros((BLOCK, HD), jnp.float32)
        picked_v = jnp.zeros((BLOCK, HD), jnp.float32)
        for b in range(nblocks):
            here = slice(b * BLOCK, (b + 1) * BLOCK)
            chosen = within[to, b][:1]
            picked_k = picked_k + chosen * k[here, LIN_DEV * HD:].astype(jnp.float32)
            picked_v = picked_v + chosen * v[here, LIN_DEV * HD:].astype(jnp.float32)
        kv_out[s, :, :HD] = bf16(picked_k)
        kv_out[s, :, HD:] = bf16(picked_v)

    def fill_send(s):
        fill(s)
        kv_copy(s).start()

    loop(1, n_ctx, fill_send)
    sib_copy.start()
    fill(0)
    own_copy = pltpu.make_async_copy(kv_out.at[0], kv_in.at[me], own_sem)
    own_copy.start()

    for head in range(LIN_DEV):
        cols = slice(head * HD, (head + 1) * HD)
        device_state = jnp.zeros((HD, HD), jnp.float32)
        for b in range(nblocks):
            here = slice(b * BLOCK, (b + 1) * BLOCK)
            state = mm_tn(k[here, cols], v[here, cols])
            st_blk[b, head] = state
            device_state = device_state + state
        st_out[head] = bf16(device_state)
    loop(1, n_ctx, lambda s: st_copy(s).start())

    own_rows = pl.ds(pl.multiple_of(h * width, width), width)

    def own_product(c):
        total[part(c)] = mm(og[part(c)], w[own_rows])

    loop(0, chunks, own_product)
    loop(1, n_ctx, lambda s: st_copy(s).wait_recv())
    st_in[me] = st_out[...]
    for head in range(LIN_DEV):
        def earlier(j, state):
            return state + jnp.where(j < me, st_in[j, head].astype(jnp.float32), 0.0)

        state = lax.fori_loop(0, n_ctx, earlier, jnp.zeros((HD, HD), jnp.float32))
        for b in range(nblocks):
            state_out[b, head] = bf16(state)
            state = state + st_blk[b, head]

    for b in range(nblocks):
        scale = block_scale(me, rows, b)
        here = slice(b * BLOCK, (b + 1) * BLOCK)
        for head in range(LIN_DEV):
            cols = slice(head * HD, (head + 1) * HD)
            scores = mm_nt(q[here, cols], k[here, cols])
            weights = bf16(jnp.where(causal_mask(), scale[:, :1] * scores, 0.0))
            inside = mm(weights, v[here, cols])
            across = mm(q[here, cols], state_out[b, head])
            lin_out[here, cols] = bf16(inside + scale * across)

    par_rows = pl.ds(pl.multiple_of(par * width, width), width)
    sib_rows = pl.ds(pl.multiple_of(sib * width, width), width)
    far_rows = pl.ds(pl.multiple_of(far * width, width), width)

    sib_copy.wait_recv()

    def sib_product(c):
        total[part(c)] += mm(og_sib[part(c)], w[sib_rows])

    loop(0, chunks, sib_product)

    def forward(c):
        par_copy(c).wait_recv()
        far_copy(c).start()
        total[part(c)] += mm(og_par[part(c)], w[par_rows])

    loop(0, chunks, forward)

    def last(c):
        far_copy(c).wait_recv()
        g_out[part(c)] = bf16(total[part(c)] + mm(og_far[part(c)], w[far_rows]))

    loop(0, chunks, last)

    def finish(s):
        kv_copy(s).wait()
        st_copy(s).wait_send()

    loop(1, n_ctx, finish)

    def finish_chunk(c):
        par_copy(c).wait_send()
        far_copy(c).wait_send()

    loop(0, chunks, finish_chunk)
    sib_copy.wait_send()
    own_copy.wait()


def sparse_kernel(
    slots, usable, q, k, v, g, far0, far1, far2, far3,
    out, dq_out, dk_out, dv_out, pairs,
    probs, pair_buf, sems,
):
    b = pl.program_id(0)
    fars = (far0, far1, far2, far3)
    neg = jnp.float32(-jnp.inf)
    qb, kb, vb, gb = q[...], k[...], v[...], g[...]
    scores = jnp.where(causal_mask(), mm_nt(qb, kb), neg)
    probs[0] = scores
    peak = jnp.max(scores, axis=1, keepdims=True)
    for r in range(LISTED):
        bias = jnp.where(usable[b, r] != 0, jnp.float32(0.0), neg)
        scores = mm_nt(qb, fars[r][0, :, :HD]) + bias
        probs[r + 1] = scores
        peak = jnp.maximum(peak, jnp.max(scores, axis=1, keepdims=True))
    sums = jnp.zeros((BLOCK, 1), jnp.float32)
    for r in range(LISTED + 1):
        e = jnp.exp((probs[r] - peak) * SCALING)
        probs[r] = e
        sums = sums + jnp.sum(e, axis=1, keepdims=True)
    inv = 1.0 / sums
    result = jnp.zeros((BLOCK, HD), jnp.float32)
    for r in range(LISTED + 1):
        prob = probs[r] * inv
        probs[r] = prob
        weight = bf16(prob)
        val = vb if r == 0 else fars[r - 1][0, :, HD:]
        result = result + mm(weight, val)
        dv = mm_tn(weight, gb)
        if r == 0:
            dv_out[...] = dv
        else:
            pair_buf[r - 1, :, HD:] = bf16(dv)
    result = bf16(result)
    out[...] = result
    row_dot = jnp.sum(gb.astype(jnp.float32) * result.astype(jnp.float32), axis=1, keepdims=True)
    dq = jnp.zeros((BLOCK, HD), jnp.float32)
    for r in range(LISTED + 1):
        val = vb if r == 0 else fars[r - 1][0, :, HD:]
        key = kb if r == 0 else fars[r - 1][0, :, :HD]
        ds = bf16(probs[r] * (mm_nt(gb, val) - row_dot))
        dq = dq + mm(ds, key)
        dk = SCALING * mm_tn(ds, qb)
        if r == 0:
            dk_out[...] = dk
        else:
            pair_buf[r - 1, :, :HD] = bf16(dk)
    dq_out[...] = bf16(SCALING * dq)
    copies = [
        pltpu.make_async_copy(pair_buf.at[r], pairs.at[slots[b, r]], sems.at[r]) for r in range(LISTED)
    ]
    for copy in copies:
        copy.start()
    for copy in copies:
        copy.wait()


def scatter_kernel(
    n_ctx, back, q, k, v, g, w, lin, sp, state, dq_sp, dk_sp, dv_sp, pairs,
    layer, dq_out, dk_out, dv_out,
    ret, att, to_far, from_far, to_par, from_par, to_sib, from_sib, own, adj_blk, adj_out, adj_in, adj,
    ret_send, ret_recv, adj_send, adj_recv, far_send, far_recv, par_send, par_recv, sib_send, sib_recv, own_sem,
):
    me = lax.axis_index("ctx")
    h = lax.axis_index("head")
    sib = h + 1 - 2 * lax.rem(h, 2)
    par = lax.rem(h + 2, 4)
    far = lax.rem(sib + 2, 4)
    rows, width = own.shape
    nblocks = rows // BLOCK
    chunks = rows // CHUNK
    enter(n_ctx, me, sib, par)

    def part(c):
        return pl.ds(pl.multiple_of(c * CHUNK, CHUNK), CHUNK)

    def loop(first, last, step):
        def body(i, carry):
            step(i)
            return carry

        lax.fori_loop(first, last, body, 0)

    def ret_copy(s):
        to = lax.rem(me + s, n_ctx)
        return remote(pairs.at[to], ret.at[me], ret_send.at[s], ret_recv.at[s], {"ctx": to})

    def adj_copy(s):
        to = lax.rem(me + s, n_ctx)
        return remote(adj_out, adj_in.at[me], adj_send.at[s], adj_recv.at[s], {"ctx": to})

    def far_copy(c):
        return remote(to_far.at[part(c)], from_far.at[part(c)], far_send.at[c], far_recv.at[c], {"head": sib})

    def par_copy(c):
        return remote(to_par.at[part(c)], from_par.at[part(c)], par_send.at[c], par_recv.at[c], {"head": par})

    def sib_copy(c):
        return remote(to_sib.at[part(c)], from_sib.at[part(c)], sib_send.at[c], sib_recv.at[c], {"head": sib})

    loop(1, n_ctx, lambda s: ret_copy(s).start())
    own_copy = pltpu.make_async_copy(pairs.at[me], ret.at[me], own_sem)
    own_copy.start()
    att[:, :LIN_DEV * HD] = lin[...]
    att[:, LIN_DEV * HD:] = sp[...]

    def product(c, dest):
        return mm_nt(att[part(c)], w[pl.ds(pl.multiple_of(dest * width, width), width)])

    def far_step(c):
        to_far[part(c)] = bf16(product(c, far))
        far_copy(c).start()

    loop(0, chunks, far_step)

    def par_step(c):
        mine = product(c, par)
        far_copy(c).wait_recv()
        to_par[part(c)] = bf16(mine + from_far[part(c)].astype(jnp.float32))
        par_copy(c).start()

    loop(0, chunks, par_step)

    for head in range(LIN_DEV):
        cols = slice(head * HD, (head + 1) * HD)
        device_adj = jnp.zeros((HD, HD), jnp.float32)
        for b in range(nblocks):
            here = slice(b * BLOCK, (b + 1) * BLOCK)
            scaled = bf16(block_scale(me, rows, b) * g[here, cols].astype(jnp.float32))
            one = mm_tn(q[here, cols], scaled)
            adj_blk[b, head] = one
            device_adj = device_adj + one
        adj_out[head] = bf16(device_adj)
    loop(1, n_ctx, lambda s: adj_copy(s).start())

    def sib_step(c):
        to_sib[part(c)] = bf16(product(c, sib))
        sib_copy(c).start()

    loop(0, chunks, sib_step)

    def own_step(c):
        own[part(c)] = product(c, h)

    loop(0, chunks, own_step)

    loop(1, n_ctx, lambda s: adj_copy(s).wait_recv())
    adj_in[me] = adj_out[...]
    for head in range(LIN_DEV):
        def later(j, total):
            return total + jnp.where(j > me, adj_in[j, head].astype(jnp.float32), 0.0)

        total = lax.fori_loop(0, n_ctx, later, jnp.zeros((HD, HD), jnp.float32))
        for b in reversed(range(nblocks)):
            adj[b, head] = bf16(total)
            total = total + adj_blk[b, head]

    for b in range(nblocks):
        scale = block_scale(me, rows, b)
        here = slice(b * BLOCK, (b + 1) * BLOCK)
        for head in range(LIN_DEV):
            cols = slice(head * HD, (head + 1) * HD)
            qb, kb, vb, gb = q[here, cols], k[here, cols], v[here, cols], g[here, cols]
            keep = causal_mask()
            weights = bf16(jnp.where(keep, scale[:, :1] * mm_nt(qb, kb), 0.0))
            grads = bf16(jnp.where(keep, scale[:, :1] * mm_nt(gb, vb), 0.0))
            dq_out[here, cols] = bf16(mm(grads, kb) + scale * mm_nt(gb, state[b, head]))
            dk_out[here, cols] = bf16(mm_tn(grads, qb) + mm_nt(vb, adj[b, head]))
            dv_out[here, cols] = bf16(mm_tn(weights, gb) + mm(kb, adj[b, head]))
        dq_out[here, LIN_DEV * HD:] = dq_sp[here]

    own_copy.wait()
    loop(1, n_ctx, lambda s: ret_copy(s).wait())
    last = slice(LIN_DEV * HD, (LIN_DEV + 1) * HD)
    for b in range(nblocks):
        for t in range(BLOCK // HD):
            here = slice(t * HD, (t + 1) * HD)
            place = slice(b * BLOCK + t * HD, b * BLOCK + (t + 1) * HD)

            def add(j, sums):
                mine = back[j][:1] == b
                got = ret[j, here].astype(jnp.float32)
                return sums + jnp.where(mine, got, 0.0)

            sums = lax.fori_loop(0, n_ctx, add, jnp.zeros((HD, 2 * HD), jnp.float32))
            dk_out[place, last] = bf16(dk_sp[place] + sums[:, :HD])
            dv_out[place, last] = bf16(dv_sp[place] + sums[:, HD:])

    def final(c):
        sib_copy(c).wait()
        par_copy(c).wait()
        far_copy(c).wait_send()
        layer[part(c)] = bf16(
            own[part(c)] + from_sib[part(c)].astype(jnp.float32) + from_par[part(c)].astype(jnp.float32)
        )

    loop(0, chunks, final)
    loop(1, n_ctx, lambda s: adj_copy(s).wait_send())


def local(queries, keys, values, out_weight, out_grad, long_blocks):
    rows = queries.shape[0]
    nblocks = rows // BLOCK
    n_ctx = lax.axis_size("ctx")
    me = lax.axis_index("ctx")
    width = out_grad.shape[1]
    chunks = rows // CHUNK
    wide = LIN_DEV * HD
    requests = LISTED * nblocks
    table = long_blocks.reshape(n_ctx, requests)
    owners = table // nblocks
    inner = table % nblocks
    aimed = owners == me
    within = jnp.sum(jnp.where(aimed, inner, 0), axis=1).astype(jnp.int32)
    back = jnp.where(jnp.any(aimed, axis=1), within, -1).astype(jnp.int32)
    within = (within[:, None] == jnp.arange(nblocks)[None, :]).astype(jnp.float32)
    within = jnp.broadcast_to(within[:, :, None, None], (n_ctx, nblocks, 8, HD))
    back = jnp.broadcast_to(back[:, None, None], (n_ctx, 8, 2 * HD))
    lists = lax.dynamic_index_in_dim(table, me, 0, False).reshape(nblocks, LISTED)
    slots = (lists // nblocks).astype(jnp.int32)
    own_index = me * nblocks + jnp.arange(nblocks, dtype=jnp.int32)
    usable = (lists != own_index[:, None]).astype(jnp.int32)

    vmem = pl.BlockSpec(memory_space=pltpu.VMEM)
    anywhere = pl.BlockSpec(memory_space=pl.ANY)
    b16, f32 = jnp.bfloat16, jnp.float32
    dma = pltpu.SemaphoreType.DMA

    attn_grad, lin_out, state, kv_in = pl.pallas_call(
        functools.partial(gather_kernel, n_ctx),
        name="gather",
        out_shape=(
            jax.ShapeDtypeStruct((rows, wide + HD), b16),
            jax.ShapeDtypeStruct((rows, wide), b16),
            jax.ShapeDtypeStruct((nblocks, LIN_DEV, HD, HD), b16),
            jax.ShapeDtypeStruct((n_ctx, BLOCK, 2 * HD), b16),
        ),
        in_specs=[vmem] * 6,
        out_specs=(vmem, vmem, vmem, anywhere),
        scratch_shapes=[
            pltpu.VMEM((rows, width), b16),
            pltpu.VMEM((rows, width), b16),
            pltpu.VMEM((rows, width), b16),
            pltpu.VMEM((n_ctx, BLOCK, 2 * HD), b16),
            pltpu.VMEM((nblocks, LIN_DEV, HD, HD), f32),
            pltpu.VMEM((LIN_DEV, HD, HD), b16),
            pltpu.VMEM((n_ctx, LIN_DEV, HD, HD), b16),
            pltpu.VMEM((rows, wide + HD), f32),
            dma((2,)),
            dma((chunks,)),
            dma((chunks,)),
            dma((chunks,)),
            dma((chunks,)),
            dma((n_ctx,)),
            dma((n_ctx,)),
            dma((n_ctx,)),
            dma((n_ctx,)),
            dma(()),
        ],
        compiler_params=pltpu.CompilerParams(
            collective_id=0, has_side_effects=True, vmem_limit_bytes=VMEM_LIMIT
        ),
    )(within, queries, keys, values, out_grad, out_weight)

    column = pl.BlockSpec((BLOCK, HD), lambda b, slots, usable: (b, LIN_DEV))
    single = pl.BlockSpec((BLOCK, HD), lambda b, slots, usable: (b, 0))

    def far_spec(r):
        return pl.BlockSpec((1, BLOCK, 2 * HD), lambda b, slots, usable: (slots[b, r], 0, 0))

    sparse_out, dq_sp, dk_sp, dv_sp, pairs = pl.pallas_call(
        sparse_kernel,
        name="sparse",
        out_shape=(
            jax.ShapeDtypeStruct((rows, HD), b16),
            jax.ShapeDtypeStruct((rows, HD), b16),
            jax.ShapeDtypeStruct((rows, HD), f32),
            jax.ShapeDtypeStruct((rows, HD), f32),
            jax.ShapeDtypeStruct((n_ctx, BLOCK, 2 * HD), b16),
        ),
        grid_spec=pltpu.PrefetchScalarGridSpec(
            num_scalar_prefetch=2,
            grid=(nblocks,),
            in_specs=[column] * 4 + [far_spec(r) for r in range(LISTED)],
            out_specs=(single, single, single, single, anywhere),
            scratch_shapes=[
                pltpu.VMEM((LISTED + 1, BLOCK, BLOCK), f32),
                pltpu.VMEM((LISTED, BLOCK, 2 * HD), b16),
                dma((LISTED,)),
            ],
        ),
        compiler_params=pltpu.CompilerParams(vmem_limit_bytes=VMEM_LIMIT),
    )(slots, usable, queries, keys, values, attn_grad, kv_in, kv_in, kv_in, kv_in)

    big = pltpu.VMEM((rows, width), b16)
    return pl.pallas_call(
        functools.partial(scatter_kernel, n_ctx),
        name="scatter",
        out_shape=(
            jax.ShapeDtypeStruct((rows, width), b16),
            jax.ShapeDtypeStruct((rows, wide + HD), b16),
            jax.ShapeDtypeStruct((rows, wide + HD), b16),
            jax.ShapeDtypeStruct((rows, wide + HD), b16),
        ),
        in_specs=[vmem] * 12 + [anywhere],
        out_specs=(vmem, vmem, vmem, vmem),
        scratch_shapes=[
            pltpu.VMEM((n_ctx, BLOCK, 2 * HD), b16),
            pltpu.VMEM((rows, wide + HD), b16),
            big, big, big, big, big, big,
            pltpu.VMEM((rows, width), f32),
            pltpu.VMEM((nblocks, LIN_DEV, HD, HD), f32),
            pltpu.VMEM((LIN_DEV, HD, HD), b16),
            pltpu.VMEM((n_ctx, LIN_DEV, HD, HD), b16),
            pltpu.VMEM((nblocks, LIN_DEV, HD, HD), b16),
            dma((n_ctx,)),
            dma((n_ctx,)),
            dma((n_ctx,)),
            dma((n_ctx,)),
            dma((chunks,)),
            dma((chunks,)),
            dma((chunks,)),
            dma((chunks,)),
            dma((chunks,)),
            dma((chunks,)),
            dma(()),
        ],
        compiler_params=pltpu.CompilerParams(
            collective_id=1, has_side_effects=True, vmem_limit_bytes=VMEM_LIMIT
        ),
    )(
        back, queries, keys, values, attn_grad, out_weight, lin_out, sparse_out, state,
        dq_sp, dk_sp, dv_sp, pairs,
    )


def solution(mesh):
    return jax.shard_map(
        local,
        mesh=mesh,
        in_specs=(
            P("ctx", "head"),
            P("ctx", "head"),
            P("ctx", "head"),
            P(None, "head"),
            P("ctx", "head"),
            P(),
        ),
        out_specs=(P("ctx", "head"), P("ctx", "head"), P("ctx", "head"), P("ctx", "head")),
        check_vma=False,
    )
```

profile of v0, /device:TPU:8, one launch (start us, length us, event | category | flops | bytes accessed | tf_op | source)
XLA Modules:
  0.0 188.4 jit_solution(11103138815681243893)
XLA Ops:
  0.6 0.7 fusion.3
  1.4 0.1 reduce_or.14
  1.5 0.1 reduce_or.18
  1.6 0.1 reduce_sum.14
  1.7 0.1 reduce_sum.18
  1.8 0.1 fusion
  1.9 0.8 copy.11
  2.6 0.1 reshape.48
  2.7 0.1 reshape.49
  2.8 0.6 compare_convert_fusion.usable
  3.4 0.6 and_select_fusion.slots
  4.0 0.7 broadcast_in_dim.12.within
  4.7 0.7 broadcast_in_dim.11.back
  5.4 78.9 %gather.1 = (bf16[1024,512]{1,0:T(8,128)(2,1)}, bf16[1024,384]{1,0:T(8,128)(2,1)}, bf16[2,3,128,128]{3,2,1,0:T(8,128)(2,1)}, bf16[8,512,256]{2,1,0:T(8,128)(2,1)}) custom-call(f32[8,2,8,128]{3,2,1,0:T(8,128)} %broadcast_in_dim.12.within, bf16[1024,512]{1,0:T(8,128)(2,1)} %q.5, bf16[1024,512]{1,0:T(8,128)(2,1)} %k.5, bf16[1024,512]{1,0:T(8,128)(2,1)} %v.5, ...), custom_call_target="tpu_custom_call" | custom-call | tf_op jit(solution)/shard_map/gather/pallas_call | solution.py:444
  84.3 16.1 %sparse.1 = (bf16[1024,128]{1,0:T(8,128)(2,1)}, bf16[1024,128]{1,0:T(8,128)(2,1)}, f32[1024,128]{1,0:T(8,128)}, f32[1024,128]{1,0:T(8,128)}, bf16[8,512,256]{2,1,0:T(8,128)(2,1)}) custom-call(s32[2,4]{1,0:T(2,128)} %and_select_fusion.slots, s32[2,4]{1,0:T(2,128)} %compare_convert_fusion.usable, bf16[1024,512]{1,0:T(8,128)(2,1)} %q.5, bf16[1024,512]{1,0:T(8,128)(2,1)} %k.5, ...), custom_call_target="tpu_custom_call" | custom-call | tf_op jit(solution)/shard_map/sparse/pallas_call | solution.py:486
  100.4 81.2 %scatter.1 = (bf16[1024,1024]{1,0:T(8,128)(2,1)}, bf16[1024,512]{1,0:T(8,128)(2,1)}, bf16[1024,512]{1,0:T(8,128)(2,1)}, bf16[1024,512]{1,0:T(8,128)(2,1)}) custom-call(s32[8,8,256]{2,1,0:T(8,128)} %broadcast_in_dim.11.back, bf16[1024,512]{1,0:T(8,128)(2,1)} %q.5, bf16[1024,512]{1,0:T(8,128)(2,1)} %k.5, bf16[1024,512]{1,0:T(8,128)(2,1)} %v.5, ...), custom_call_target="tpu_custom_call" | custom-call | tf_op jit(solution)/shard_map/scatter/pallas_call | solution.py:511
  181.7 0.0 copy-start.2
  181.7 3.2 %copy.16 = bf16[1024,1024]{1,0:T(8,128)(2,1)} copy(bf16[1024,1024]{1,0:T(8,128)(2,1)} %get-tuple-element.28) | data formatting | bytes 4194304
  184.8 0.0 copy-done.2
  184.8 0.0 copy-start.1
  184.8 0.0 copy-start
  184.8 1.0 copy.17
  185.8 0.6 copy-done.1
  186.4 1.0 copy.18
  187.4 0.0 copy-done
  187.4 1.0 copy.19
  (4 shorter events, 0.1 us)
Async XLA Ops:
  181.7 3.2 %copy-start.2 = (bf16[1024,512]{1,0:T(8,128)(2,1)S(1)}, bf16[1024,512]{1,0:T(8,128)(2,1)}, u32[]{:S(2)}) copy-start(bf16[1024,512]{1,0:T(8,128)(2,1)} %get-tuple-element.29) | copy-start | bytes 3145732
  184.8 1.6 copy-start.1
  184.8 2.6 %copy-start = (bf16[1024,512]{1,0:T(8,128)(2,1)S(1)}, bf16[1024,512]{1,0:T(8,128)(2,1)}, u32[]{:S(2)}) copy-start(bf16[1024,512]{1,0:T(8,128)(2,1)} %get-tuple-element.31) | copy-start | bytes 3145732
where the time goes:
time: 191 us; the launch traced here: 188 us
  Pallas kernels  176 us (92%)
  local copies, waits for them, and re-layouts  9.23 us (5%)
  other arithmetic  2.25 us (1%)
    pallas_call x1, Pallas kernels, local(): pl.pallas_call(functools.partial(scatter_kernel, n_ctx), name='scatter',...  81.2 us
    pallas_call x1, Pallas kernels, local(): pl.pallas_call(functools.partial(gather_kernel, n_ctx), name='gather', ou...  78.9 us
    pallas_call x1, Pallas kernels, local(): pl.pallas_call(sparse_kernel, name='sparse', out_shape=(jax.ShapeDtypeStr...  16.1 us
    unnamed x11, local copies, waits for them, and re-layouts  7.48 us

commit v1 on v0

--- a/solution.py
+++ b/solution.py
@@ -67,10 +67,66 @@
     pl.semaphore_wait(barrier, n_ctx + 1)
 
 
+def asked(table, place, block, nblocks):
+    count = jnp.int32(0)
+    for i in range(nblocks):
+        for r in range(LISTED):
+            count = count + (table[place * nblocks + i, r] == block).astype(jnp.int32)
+    return count
+
+
+class Scan:
+    def __init__(self, n_ctx, me, backward, own, total, out, arrived, send, recv):
+        self.n_ctx, self.me, self.backward = n_ctx, me, backward
+        self.own, self.total, self.out, self.arrived = own, total, out, arrived
+        self.send, self.recv = send, recv
+        self.steps = (n_ctx - 1).bit_length()
+
+    def copy(self, i):
+        shift = self.n_ctx - (1 << i) if self.backward else 1 << i
+        to = lax.rem(self.me + shift, self.n_ctx)
+        return remote(self.out.at[i], self.arrived.at[i], self.send.at[i], self.recv.at[i], {"ctx": to})
+
+    def sends(self, i):
+        return self.me >= (1 << i) if self.backward else self.me < self.n_ctx - (1 << i)
+
+    def receives(self, i):
+        return self.me < self.n_ctx - (1 << i) if self.backward else self.me >= (1 << i)
+
+    def begin(self):
+        self.total[...] = jnp.zeros_like(self.total)
+        self.start(0)
+
+    def start(self, i):
+        self.out[i] = bf16(self.own[...] + self.total[...])
+
+        @pl.when(self.sends(i))
+        def _():
+            self.copy(i).start()
+
+    def receive(self, i):
+        @pl.when(self.receives(i))
+        def _():
+            self.copy(i).wait_recv()
+            self.total[...] += self.arrived[i].astype(jnp.float32)
+
+    def advance(self, i):
+        if i < self.steps:
+            self.receive(i)
+            if i + 1 < self.steps:
+                self.start(i + 1)
+
+    def finish(self):
+        for i in range(self.steps):
+            @pl.when(self.sends(i))
+            def _():
+                self.copy(i).wait_send()
+
+
 def gather_kernel(
-    n_ctx, within, q, k, v, og, w,
+    n_ctx, table, q, k, v, og, w,
     g_out, lin_out, state_out, kv_in,
-    og_sib, og_par, og_far, kv_out, st_blk, st_out, st_in, total,
+    og_sib, og_par, og_far, kv_out, st_blk, st_own, st_sum, st_out, st_in, total,
     sib_sems, par_send, par_recv, far_send, far_recv, kv_send, kv_recv, st_send, st_recv, own_sem,
 ):
     me = lax.axis_index("ctx")
@@ -98,9 +154,7 @@
         to = lax.rem(me + s, n_ctx)
         return remote(kv_out.at[s], kv_in.at[me], kv_send.at[s], kv_recv.at[s], {"ctx": to})
 
-    def st_copy(s):
-        to = lax.rem(me + s, n_ctx)
-        return remote(st_out, st_in.at[me], st_send.at[s], st_recv.at[s], {"ctx": to})
+    scan = Scan(n_ctx, me, False, st_own, st_sum, st_out, st_in, st_send, st_recv)
 
     def loop(first, last, step):
         def body(i, carry):
@@ -117,7 +171,7 @@
         picked_v = jnp.zeros((BLOCK, HD), jnp.float32)
         for b in range(nblocks):
             here = slice(b * BLOCK, (b + 1) * BLOCK)
-            chosen = within[to, b][:1]
+            chosen = asked(table, to, me * nblocks + b, nblocks).astype(jnp.float32)
             picked_k = picked_k + chosen * k[here, LIN_DEV * HD:].astype(jnp.float32)
             picked_v = picked_v + chosen * v[here, LIN_DEV * HD:].astype(jnp.float32)
         kv_out[s, :, :HD] = bf16(picked_k)
@@ -141,8 +195,8 @@
             state = mm_tn(k[here, cols], v[here, cols])
             st_blk[b, head] = state
             device_state = device_state + state
-        st_out[head] = bf16(device_state)
-    loop(1, n_ctx, lambda s: st_copy(s).start())
+        st_own[head] = device_state
+    scan.begin()
 
     own_rows = pl.ds(pl.multiple_of(h * width, width), width)
 
@@ -150,13 +204,18 @@
         total[part(c)] = mm(og[part(c)], w[own_rows])
 
     loop(0, chunks, own_product)
-    loop(1, n_ctx, lambda s: st_copy(s).wait_recv())
-    st_in[me] = st_out[...]
+    scan.advance(0)
+    sib_rows = pl.ds(pl.multiple_of(sib * width, width), width)
+    sib_copy.wait_recv()
+
+    def sib_product(c):
+        total[part(c)] += mm(og_sib[part(c)], w[sib_rows])
+
+    loop(0, chunks, sib_product)
+    for i in range(1, scan.steps):
+        scan.advance(i)
     for head in range(LIN_DEV):
-        def earlier(j, state):
-            return state + jnp.where(j < me, st_in[j, head].astype(jnp.float32), 0.0)
-
-        state = lax.fori_loop(0, n_ctx, earlier, jnp.zeros((HD, HD), jnp.float32))
+        state = st_sum[head]
         for b in range(nblocks):
             state_out[b, head] = bf16(state)
             state = state + st_blk[b, head]
@@ -173,15 +232,7 @@
             lin_out[here, cols] = bf16(inside + scale * across)
 
     par_rows = pl.ds(pl.multiple_of(par * width, width), width)
-    sib_rows = pl.ds(pl.multiple_of(sib * width, width), width)
     far_rows = pl.ds(pl.multiple_of(far * width, width), width)
-
-    sib_copy.wait_recv()
-
-    def sib_product(c):
-        total[part(c)] += mm(og_sib[part(c)], w[sib_rows])
-
-    loop(0, chunks, sib_product)
 
     def forward(c):
         par_copy(c).wait_recv()
@@ -196,11 +247,8 @@
 
     loop(0, chunks, last)
 
-    def finish(s):
-        kv_copy(s).wait()
-        st_copy(s).wait_send()
-
-    loop(1, n_ctx, finish)
+    loop(1, n_ctx, lambda s: kv_copy(s).wait())
+    scan.finish()
 
     def finish_chunk(c):
         par_copy(c).wait_send()
@@ -212,11 +260,13 @@
 
 
 def sparse_kernel(
-    slots, usable, q, k, v, g, far0, far1, far2, far3,
+    table, place, q, k, v, g, far0, far1, far2, far3,
     out, dq_out, dk_out, dv_out, pairs,
     probs, pair_buf, sems,
 ):
     b = pl.program_id(0)
+    nblocks = pl.num_programs(0)
+    here = place[0] * nblocks + b
     fars = (far0, far1, far2, far3)
     neg = jnp.float32(-jnp.inf)
     qb, kb, vb, gb = q[...], k[...], v[...], g[...]
@@ -224,7 +274,7 @@
     probs[0] = scores
     peak = jnp.max(scores, axis=1, keepdims=True)
     for r in range(LISTED):
-        bias = jnp.where(usable[b, r] != 0, jnp.float32(0.0), neg)
+        bias = jnp.where(table[here, r] != here, jnp.float32(0.0), neg)
         scores = mm_nt(qb, fars[r][0, :, :HD]) + bias
         probs[r + 1] = scores
         peak = jnp.maximum(peak, jnp.max(scores, axis=1, keepdims=True))
@@ -262,7 +312,7 @@
             pair_buf[r - 1, :, :HD] = bf16(dk)
     dq_out[...] = bf16(SCALING * dq)
     copies = [
-        pltpu.make_async_copy(pair_buf.at[r], pairs.at[slots[b, r]], sems.at[r]) for r in range(LISTED)
+        pltpu.make_async_copy(pair_buf.at[r], pairs.at[table[here, r] // nblocks], sems.at[r]) for r in range(LISTED)
     ]
     for copy in copies:
         copy.start()
@@ -271,9 +321,9 @@
 
 
 def scatter_kernel(
-    n_ctx, back, q, k, v, g, w, lin, sp, state, dq_sp, dk_sp, dv_sp, pairs,
+    n_ctx, table, q, k, v, g, w, lin, sp, state, dq_sp, dk_sp, dv_sp, pairs,
     layer, dq_out, dk_out, dv_out,
-    ret, att, to_far, from_far, to_par, from_par, to_sib, from_sib, own, adj_blk, adj_out, adj_in, adj,
+    ret, att, to_far, from_far, to_par, from_par, to_sib, from_sib, own, adj_blk, adj_own, adj_sum, adj_out, adj_in, adj,
     ret_send, ret_recv, adj_send, adj_recv, far_send, far_recv, par_send, par_recv, sib_send, sib_recv, own_sem,
 ):
     me = lax.axis_index("ctx")
@@ -300,9 +350,7 @@
         to = lax.rem(me + s, n_ctx)
         return remote(pairs.at[to], ret.at[me], ret_send.at[s], ret_recv.at[s], {"ctx": to})
 
-    def adj_copy(s):
-        to = lax.rem(me + s, n_ctx)
-        return remote(adj_out, adj_in.at[me], adj_send.at[s], adj_recv.at[s], {"ctx": to})
+    scan = Scan(n_ctx, me, True, adj_own, adj_sum, adj_out, adj_in, adj_send, adj_recv)
 
     def far_copy(c):
         return remote(to_far.at[part(c)], from_far.at[part(c)], far_send.at[c], far_recv.at[c], {"head": sib})
@@ -327,14 +375,6 @@
         far_copy(c).start()
 
     loop(0, chunks, far_step)
-
-    def par_step(c):
-        mine = product(c, par)
-        far_copy(c).wait_recv()
-        to_par[part(c)] = bf16(mine + from_far[part(c)].astype(jnp.float32))
-        par_copy(c).start()
-
-    loop(0, chunks, par_step)
 
     for head in range(LIN_DEV):
         cols = slice(head * HD, (head + 1) * HD)
@@ -345,27 +385,35 @@
             one = mm_tn(q[here, cols], scaled)
             adj_blk[b, head] = one
             device_adj = device_adj + one
-        adj_out[head] = bf16(device_adj)
-    loop(1, n_ctx, lambda s: adj_copy(s).start())
+        adj_own[head] = device_adj
+    scan.begin()
+
+    def par_step(c):
+        mine = product(c, par)
+        far_copy(c).wait_recv()
+        to_par[part(c)] = bf16(mine + from_far[part(c)].astype(jnp.float32))
+        par_copy(c).start()
+
+    loop(0, chunks, par_step)
+
+    scan.advance(0)
 
     def sib_step(c):
         to_sib[part(c)] = bf16(product(c, sib))
         sib_copy(c).start()
 
     loop(0, chunks, sib_step)
+    scan.advance(1)
 
     def own_step(c):
         own[part(c)] = product(c, h)
 
     loop(0, chunks, own_step)
 
-    loop(1, n_ctx, lambda s: adj_copy(s).wait_recv())
-    adj_in[me] = adj_out[...]
+    for i in range(2, scan.steps):
+        scan.advance(i)
     for head in range(LIN_DEV):
-        def later(j, total):
-            return total + jnp.where(j > me, adj_in[j, head].astype(jnp.float32), 0.0)
-
-        total = lax.fori_loop(0, n_ctx, later, jnp.zeros((HD, HD), jnp.float32))
+        total = adj_sum[head]
         for b in reversed(range(nblocks)):
             adj[b, head] = bf16(total)
             total = total + adj_blk[b, head]
@@ -393,7 +441,7 @@
             place = slice(b * BLOCK + t * HD, b * BLOCK + (t + 1) * HD)
 
             def add(j, sums):
-                mine = back[j][:1] == b
+                mine = jnp.full((1, 2 * HD), asked(table, j, me * nblocks + b, nblocks), jnp.int32) > 0
                 got = ret[j, here].astype(jnp.float32)
                 return sums + jnp.where(mine, got, 0.0)
 
@@ -410,32 +458,20 @@
         )
 
     loop(0, chunks, final)
-    loop(1, n_ctx, lambda s: adj_copy(s).wait_send())
+    scan.finish()
 
 
 def local(queries, keys, values, out_weight, out_grad, long_blocks):
     rows = queries.shape[0]
     nblocks = rows // BLOCK
     n_ctx = lax.axis_size("ctx")
-    me = lax.axis_index("ctx")
+    place = lax.axis_index("ctx").astype(jnp.int32).reshape(1)
     width = out_grad.shape[1]
     chunks = rows // CHUNK
     wide = LIN_DEV * HD
-    requests = LISTED * nblocks
-    table = long_blocks.reshape(n_ctx, requests)
-    owners = table // nblocks
-    inner = table % nblocks
-    aimed = owners == me
-    within = jnp.sum(jnp.where(aimed, inner, 0), axis=1).astype(jnp.int32)
-    back = jnp.where(jnp.any(aimed, axis=1), within, -1).astype(jnp.int32)
-    within = (within[:, None] == jnp.arange(nblocks)[None, :]).astype(jnp.float32)
-    within = jnp.broadcast_to(within[:, :, None, None], (n_ctx, nblocks, 8, HD))
-    back = jnp.broadcast_to(back[:, None, None], (n_ctx, 8, 2 * HD))
-    lists = lax.dynamic_index_in_dim(table, me, 0, False).reshape(nblocks, LISTED)
-    slots = (lists // nblocks).astype(jnp.int32)
-    own_index = me * nblocks + jnp.arange(nblocks, dtype=jnp.int32)
-    usable = (lists != own_index[:, None]).astype(jnp.int32)
-
+    steps = (n_ctx - 1).bit_length()
+
+    smem = pl.BlockSpec(memory_space=pltpu.SMEM)
     vmem = pl.BlockSpec(memory_space=pltpu.VMEM)
     anywhere = pl.BlockSpec(memory_space=pl.ANY)
     b16, f32 = jnp.bfloat16, jnp.float32
@@ -450,7 +486,7 @@
             jax.ShapeDtypeStruct((nblocks, LIN_DEV, HD, HD), b16),
             jax.ShapeDtypeStruct((n_ctx, BLOCK, 2 * HD), b16),
         ),
-        in_specs=[vmem] * 6,
+        in_specs=[smem] + [vmem] * 5,
         out_specs=(vmem, vmem, vmem, anywhere),
         scratch_shapes=[
             pltpu.VMEM((rows, width), b16),
@@ -458,8 +494,10 @@
             pltpu.VMEM((rows, width), b16),
             pltpu.VMEM((n_ctx, BLOCK, 2 * HD), b16),
             pltpu.VMEM((nblocks, LIN_DEV, HD, HD), f32),
-            pltpu.VMEM((LIN_DEV, HD, HD), b16),
-            pltpu.VMEM((n_ctx, LIN_DEV, HD, HD), b16),
+            pltpu.VMEM((LIN_DEV, HD, HD), f32),
+            pltpu.VMEM((LIN_DEV, HD, HD), f32),
+            pltpu.VMEM((steps, LIN_DEV, HD, HD), b16),
+            pltpu.VMEM((steps, LIN_DEV, HD, HD), b16),
             pltpu.VMEM((rows, wide + HD), f32),
             dma((2,)),
             dma((chunks,)),
@@ -468,20 +506,20 @@
             dma((chunks,)),
             dma((n_ctx,)),
             dma((n_ctx,)),
-            dma((n_ctx,)),
-            dma((n_ctx,)),
+            dma((steps,)),
+            dma((steps,)),
             dma(()),
         ],
         compiler_params=pltpu.CompilerParams(
             collective_id=0, has_side_effects=True, vmem_limit_bytes=VMEM_LIMIT
         ),
-    )(within, queries, keys, values, out_grad, out_weight)
-
-    column = pl.BlockSpec((BLOCK, HD), lambda b, slots, usable: (b, LIN_DEV))
-    single = pl.BlockSpec((BLOCK, HD), lambda b, slots, usable: (b, 0))
+    )(long_blocks, queries, keys, values, out_grad, out_weight)
+
+    column = pl.BlockSpec((BLOCK, HD), lambda b, table, place: (b, LIN_DEV))
+    single = pl.BlockSpec((BLOCK, HD), lambda b, table, place: (b, 0))
 
     def far_spec(r):
-        return pl.BlockSpec((1, BLOCK, 2 * HD), lambda b, slots, usable: (slots[b, r], 0, 0))
+        return pl.BlockSpec((1, BLOCK, 2 * HD), lambda b, table, place: (table[place[0] * nblocks + b, r] // nblocks, 0, 0))
 
     sparse_out, dq_sp, dk_sp, dv_sp, pairs = pl.pallas_call(
         sparse_kernel,
@@ -505,7 +543,7 @@
             ],
         ),
         compiler_params=pltpu.CompilerParams(vmem_limit_bytes=VMEM_LIMIT),
-    )(slots, usable, queries, keys, values, attn_grad, kv_in, kv_in, kv_in, kv_in)
+    )(long_blocks, place, queries, keys, values, attn_grad, kv_in, kv_in, kv_in, kv_in)
 
     big = pltpu.VMEM((rows, width), b16)
     return pl.pallas_call(
@@ -517,7 +555,7 @@
             jax.ShapeDtypeStruct((rows, wide + HD), b16),
             jax.ShapeDtypeStruct((rows, wide + HD), b16),
         ),
-        in_specs=[vmem] * 12 + [anywhere],
+        in_specs=[smem] + [vmem] * 11 + [anywhere],
         out_specs=(vmem, vmem, vmem, vmem),
         scratch_shapes=[
             pltpu.VMEM((n_ctx, BLOCK, 2 * HD), b16),
@@ -525,13 +563,15 @@
             big, big, big, big, big, big,
             pltpu.VMEM((rows, width), f32),
             pltpu.VMEM((nblocks, LIN_DEV, HD, HD), f32),
-            pltpu.VMEM((LIN_DEV, HD, HD), b16),
-            pltpu.VMEM((n_ctx, LIN_DEV, HD, HD), b16),
+            pltpu.VMEM((LIN_DEV, HD, HD), f32),
+            pltpu.VMEM((LIN_DEV, HD, HD), f32),
+            pltpu.VMEM((steps, LIN_DEV, HD, HD), b16),
+            pltpu.VMEM((steps, LIN_DEV, HD, HD), b16),
             pltpu.VMEM((nblocks, LIN_DEV, HD, HD), b16),
             dma((n_ctx,)),
             dma((n_ctx,)),
-            dma((n_ctx,)),
-            dma((n_ctx,)),
+            dma((steps,)),
+            dma((steps,)),
             dma((chunks,)),
             dma((chunks,)),
             dma((chunks,)),
@@ -544,7 +584,7 @@
             collective_id=1, has_side_effects=True, vmem_limit_bytes=VMEM_LIMIT
         ),
     )(
-        back, queries, keys, values, attn_grad, out_weight, lin_out, sparse_out, state,
+        long_blocks, queries, keys, values, attn_grad, out_weight, lin_out, sparse_out, state,
         dq_sp, dk_sp, dv_sp, pairs,
     )
 

time: 191 us -> 171 us (0.90)
  Pallas kernels: 176 us -> 159 us
  other arithmetic: 2.25 us -> 0 us
    pallas_call x1, Pallas kernels: 78.9 us -> 60.7 us  [local(): pl.pallas_call(functools.partial(gather_kernel, n_ctx), name='gather', ou...]
where the time goes in v1:
time: 171 us; the launch traced here: 168 us
  Pallas kernels  159 us (93%)
  local copies, waits for them, and re-layouts  8.07 us (5%)
    pallas_call x1, Pallas kernels, local(): pl.pallas_call(functools.partial(scatter_kernel, n_ctx), name='scatter',...  81.8 us
    pallas_call x1, Pallas kernels, local(): pl.pallas_call(functools.partial(gather_kernel, n_ctx), name='gather', ou...  60.7 us
    pallas_call x1, Pallas kernels, local(): pl.pallas_call(sparse_kernel, name='sparse', out_shape=(jax.ShapeDtypeStr...  16.3 us
    unnamed x11, local copies, waits for them, and re-layouts  8.07 us

profile of v1, /device:TPU:8, one launch (start us, length us, event | category | flops | bytes accessed | tf_op | source)
XLA Modules:
  0.0 167.5 jit_solution(10575891904054695770)
XLA Ops:
  0.6 1.4 copy.12.table
  2.0 60.7 %gather.1 = (bf16[1024,512]{1,0:T(8,128)(2,1)}, bf16[1024,384]{1,0:T(8,128)(2,1)}, bf16[2,3,128,128]{3,2,1,0:T(8,128)(2,1)}, bf16[8,512,256]{2,1,0:T(8,128)(2,1)}) custom-call(s32[16,4]{1,0:T(8,128)} %copy.12.table, bf16[1024,512]{1,0:T(8,128)(2,1)} %q.5, bf16[1024,512]{1,0:T(8,128)(2,1)} %k.5, bf16[1024,512]{1,0:T(8,128)(2,1)} %v.5, bf16[1024,1024]{1,0:T(8,128)(2,1)} %og.1, ...), custom_call_target="tpu_custom_call" | custom-call | tf_op jit(solution)/shard_map/gather/pallas_call | solution.py:480
  62.7 16.3 %sparse.1 = (bf16[1024,128]{1,0:T(8,128)(2,1)}, bf16[1024,128]{1,0:T(8,128)(2,1)}, f32[1024,128]{1,0:T(8,128)}, f32[1024,128]{1,0:T(8,128)}, bf16[8,512,256]{2,1,0:T(8,128)(2,1)}) custom-call(s32[16,4]{1,0:T(8,128)} %copy.12.table, s32[1]{0:T(128)} %bitcast.place, bf16[1024,512]{1,0:T(8,128)(2,1)} %q.5, bf16[1024,512]{1,0:T(8,128)(2,1)} %k.5, ...), custom_call_target="tpu_custom_call" | custom-call | tf_op jit(solution)/shard_map/sparse/pallas_call | solution.py:524
  78.9 81.8 %scatter.1 = (bf16[1024,1024]{1,0:T(8,128)(2,1)}, bf16[1024,512]{1,0:T(8,128)(2,1)}, bf16[1024,512]{1,0:T(8,128)(2,1)}, bf16[1024,512]{1,0:T(8,128)(2,1)}) custom-call(s32[16,4]{1,0:T(8,128)} %copy.12.table, bf16[1024,512]{1,0:T(8,128)(2,1)} %q.5, bf16[1024,512]{1,0:T(8,128)(2,1)} %k.5, bf16[1024,512]{1,0:T(8,128)(2,1)} %v.5, ...), custom_call_target="tpu_custom_call" | custom-call | tf_op jit(solution)/shard_map/scatter/pallas_call | solution.py:549
  160.8 0.0 copy-start.2
  160.8 3.2 %copy.17 = bf16[1024,1024]{1,0:T(8,128)(2,1)} copy(bf16[1024,1024]{1,0:T(8,128)(2,1)} %get-tuple-element.26) | data formatting | bytes 4194304
  163.9 0.0 copy-done.2
  164.0 0.0 copy-start.1
  164.0 0.0 copy-start
  164.0 1.0 copy.18
  164.9 0.6 copy-done.1
  165.6 1.0 copy.19
  166.5 0.0 copy-done
  166.5 1.0 copy.20
Async XLA Ops:
  160.8 3.2 %copy-start.2 = (bf16[1024,512]{1,0:T(8,128)(2,1)S(1)}, bf16[1024,512]{1,0:T(8,128)(2,1)}, u32[]{:S(2)}) copy-start(bf16[1024,512]{1,0:T(8,128)(2,1)} %get-tuple-element.27) | copy-start | bytes 3145732
  164.0 1.6 copy-start.1
  164.0 2.6 %copy-start = (bf16[1024,512]{1,0:T(8,128)(2,1)S(1)}, bf16[1024,512]{1,0:T(8,128)(2,1)}, u32[]{:S(2)}) copy-start(bf16[1024,512]{1,0:T(8,128)(2,1)} %get-tuple-element.29) | copy-start | bytes 3145732

commit v2 on v1

--- a/solution.py
+++ b/solution.py
@@ -126,7 +126,7 @@
 def gather_kernel(
     n_ctx, table, q, k, v, og, w,
     g_out, lin_out, state_out, kv_in,
-    og_sib, og_par, og_far, kv_out, st_blk, st_own, st_sum, st_out, st_in, total,
+    og_sib, og_par, og_far, kv_out, lin_acc, st_blk, st_own, st_sum, st_out, st_in, total,
     sib_sems, par_send, par_recv, far_send, far_recv, kv_send, kv_recv, st_send, st_recv, own_sem,
 ):
     me = lax.axis_index("ctx")
@@ -181,12 +181,6 @@
         fill(s)
         kv_copy(s).start()
 
-    loop(1, n_ctx, fill_send)
-    sib_copy.start()
-    fill(0)
-    own_copy = pltpu.make_async_copy(kv_out.at[0], kv_in.at[me], own_sem)
-    own_copy.start()
-
     for head in range(LIN_DEV):
         cols = slice(head * HD, (head + 1) * HD)
         device_state = jnp.zeros((HD, HD), jnp.float32)
@@ -197,6 +191,11 @@
             device_state = device_state + state
         st_own[head] = device_state
     scan.begin()
+    loop(1, n_ctx, fill_send)
+    sib_copy.start()
+    fill(0)
+    own_copy = pltpu.make_async_copy(kv_out.at[0], kv_in.at[me], own_sem)
+    own_copy.start()
 
     own_rows = pl.ds(pl.multiple_of(h * width, width), width)
 
@@ -212,14 +211,6 @@
         total[part(c)] += mm(og_sib[part(c)], w[sib_rows])
 
     loop(0, chunks, sib_product)
-    for i in range(1, scan.steps):
-        scan.advance(i)
-    for head in range(LIN_DEV):
-        state = st_sum[head]
-        for b in range(nblocks):
-            state_out[b, head] = bf16(state)
-            state = state + st_blk[b, head]
-
     for b in range(nblocks):
         scale = block_scale(me, rows, b)
         here = slice(b * BLOCK, (b + 1) * BLOCK)
@@ -228,8 +219,7 @@
             scores = mm_nt(q[here, cols], k[here, cols])
             weights = bf16(jnp.where(causal_mask(), scale[:, :1] * scores, 0.0))
             inside = mm(weights, v[here, cols])
-            across = mm(q[here, cols], state_out[b, head])
-            lin_out[here, cols] = bf16(inside + scale * across)
+            lin_acc[here, cols] = inside
 
     par_rows = pl.ds(pl.multiple_of(par * width, width), width)
     far_rows = pl.ds(pl.multiple_of(far * width, width), width)
@@ -239,7 +229,25 @@
         far_copy(c).start()
         total[part(c)] += mm(og_par[part(c)], w[par_rows])
 
-    loop(0, chunks, forward)
+    loop(0, chunks // 2, forward)
+    scan.advance(1)
+    loop(chunks // 2, chunks, forward)
+    for i in range(2, scan.steps):
+        scan.advance(i)
+    for head in range(LIN_DEV):
+        state = st_sum[head]
+        for b in range(nblocks):
+            state_out[b, head] = bf16(state)
+            state = state + st_blk[b, head]
+
+    for b in range(nblocks):
+        scale = block_scale(me, rows, b)
+        here = slice(b * BLOCK, (b + 1) * BLOCK)
+        for head in range(LIN_DEV):
+            cols = slice(head * HD, (head + 1) * HD)
+            across = mm(q[here, cols], state_out[b, head])
+            lin_out[here, cols] = bf16(lin_acc[here, cols] + scale * across)
+
 
     def last(c):
         far_copy(c).wait_recv()
@@ -323,7 +331,7 @@
 def scatter_kernel(
     n_ctx, table, q, k, v, g, w, lin, sp, state, dq_sp, dk_sp, dv_sp, pairs,
     layer, dq_out, dk_out, dv_out,
-    ret, att, to_far, from_far, to_par, from_par, to_sib, from_sib, own, adj_blk, adj_own, adj_sum, adj_out, adj_in, adj,
+    ret, att, to_far, from_far, to_par, from_par, to_sib, from_sib, own, dk_acc, dv_acc, adj_blk, adj_own, adj_sum, adj_out, adj_in, adj,
     ret_send, ret_recv, adj_send, adj_recv, far_send, far_recv, par_send, par_recv, sib_send, sib_recv, own_sem,
 ):
     me = lax.axis_index("ctx")
@@ -361,21 +369,6 @@
     def sib_copy(c):
         return remote(to_sib.at[part(c)], from_sib.at[part(c)], sib_send.at[c], sib_recv.at[c], {"head": sib})
 
-    loop(1, n_ctx, lambda s: ret_copy(s).start())
-    own_copy = pltpu.make_async_copy(pairs.at[me], ret.at[me], own_sem)
-    own_copy.start()
-    att[:, :LIN_DEV * HD] = lin[...]
-    att[:, LIN_DEV * HD:] = sp[...]
-
-    def product(c, dest):
-        return mm_nt(att[part(c)], w[pl.ds(pl.multiple_of(dest * width, width), width)])
-
-    def far_step(c):
-        to_far[part(c)] = bf16(product(c, far))
-        far_copy(c).start()
-
-    loop(0, chunks, far_step)
-
     for head in range(LIN_DEV):
         cols = slice(head * HD, (head + 1) * HD)
         device_adj = jnp.zeros((HD, HD), jnp.float32)
@@ -387,6 +380,20 @@
             device_adj = device_adj + one
         adj_own[head] = device_adj
     scan.begin()
+    loop(1, n_ctx, lambda s: ret_copy(s).start())
+    own_copy = pltpu.make_async_copy(pairs.at[me], ret.at[me], own_sem)
+    own_copy.start()
+    att[:, :LIN_DEV * HD] = lin[...]
+    att[:, LIN_DEV * HD:] = sp[...]
+
+    def product(c, dest):
+        return mm_nt(att[part(c)], w[pl.ds(pl.multiple_of(dest * width, width), width)])
+
+    def far_step(c):
+        to_far[part(c)] = bf16(product(c, far))
+        far_copy(c).start()
+
+    loop(0, chunks, far_step)
 
     def par_step(c):
         mine = product(c, par)
@@ -403,20 +410,12 @@
         sib_copy(c).start()
 
     loop(0, chunks, sib_step)
-    scan.advance(1)
 
     def own_step(c):
         own[part(c)] = product(c, h)
 
     loop(0, chunks, own_step)
-
-    for i in range(2, scan.steps):
-        scan.advance(i)
-    for head in range(LIN_DEV):
-        total = adj_sum[head]
-        for b in reversed(range(nblocks)):
-            adj[b, head] = bf16(total)
-            total = total + adj_blk[b, head]
+    scan.advance(1)
 
     for b in range(nblocks):
         scale = block_scale(me, rows, b)
@@ -428,8 +427,8 @@
             weights = bf16(jnp.where(keep, scale[:, :1] * mm_nt(qb, kb), 0.0))
             grads = bf16(jnp.where(keep, scale[:, :1] * mm_nt(gb, vb), 0.0))
             dq_out[here, cols] = bf16(mm(grads, kb) + scale * mm_nt(gb, state[b, head]))
-            dk_out[here, cols] = bf16(mm_tn(grads, qb) + mm_nt(vb, adj[b, head]))
-            dv_out[here, cols] = bf16(mm_tn(weights, gb) + mm(kb, adj[b, head]))
+            dk_acc[here, cols] = mm_tn(grads, qb)
+            dv_acc[here, cols] = mm_tn(weights, gb)
         dq_out[here, LIN_DEV * HD:] = dq_sp[here]
 
     own_copy.wait()
@@ -458,6 +457,20 @@
         )
 
     loop(0, chunks, final)
+    for i in range(2, scan.steps):
+        scan.advance(i)
+    for head in range(LIN_DEV):
+        total = adj_sum[head]
+        for b in reversed(range(nblocks)):
+            adj[b, head] = bf16(total)
+            total = total + adj_blk[b, head]
+
+    for b in range(nblocks):
+        here = slice(b * BLOCK, (b + 1) * BLOCK)
+        for head in range(LIN_DEV):
+            cols = slice(head * HD, (head + 1) * HD)
+            dk_out[here, cols] = bf16(dk_acc[here, cols] + mm_nt(v[here, cols], adj[b, head]))
+            dv_out[here, cols] = bf16(dv_acc[here, cols] + mm(k[here, cols], adj[b, head]))
     scan.finish()
 
 
@@ -493,6 +506,7 @@
             pltpu.VMEM((rows, width), b16),
             pltpu.VMEM((rows, width), b16),
             pltpu.VMEM((n_ctx, BLOCK, 2 * HD), b16),
+            pltpu.VMEM((rows, wide), f32),
             pltpu.VMEM((nblocks, LIN_DEV, HD, HD), f32),
             pltpu.VMEM((LIN_DEV, HD, HD), f32),
             pltpu.VMEM((LIN_DEV, HD, HD), f32),
@@ -562,6 +576,8 @@
             pltpu.VMEM((rows, wide + HD), b16),
             big, big, big, big, big, big,
             pltpu.VMEM((rows, width), f32),
+            pltpu.VMEM((rows, wide), f32),
+            pltpu.VMEM((rows, wide), f32),
             pltpu.VMEM((nblocks, LIN_DEV, HD, HD), f32),
             pltpu.VMEM((LIN_DEV, HD, HD), f32),
             pltpu.VMEM((LIN_DEV, HD, HD), f32),

time: 171 us -> 162 us (0.947); the launches traced: 168 us -> 162 us
  Pallas kernels: 159 us -> 153 us
    pallas_call x1, Pallas kernels: 81.8 us -> 76.2 us  [local(): pl.pallas_call(functools.partial(scatter_kernel, n_ctx), name='scatter',...]
where the time goes in v2:
time: 162 us
  Pallas kernels  153 us (94%)
  local copies, waits for them, and re-layouts  8.07 us (5%)
    pallas_call x1, Pallas kernels, local(): pl.pallas_call(functools.partial(scatter_kernel, n_ctx), name='scatter',...  76.2 us
    pallas_call x1, Pallas kernels, local(): pl.pallas_call(functools.partial(gather_kernel, n_ctx), name='gather', ou...  61 us
    pallas_call x1, Pallas kernels, local(): pl.pallas_call(sparse_kernel, name='sparse', out_shape=(jax.ShapeDtypeStr...  16.3 us
    unnamed x11, local copies, waits for them, and re-layouts  8.07 us

profile of v2, /device:TPU:8, one launch (start us, length us, event | category | flops | bytes accessed | tf_op | source)
XLA Modules:
  0.0 162.2 jit_solution(12180210078305047577)
XLA Ops:
  0.6 1.4 copy.12.table
  2.0 61.0 %gather.1 = (bf16[1024,512]{1,0:T(8,128)(2,1)}, bf16[1024,384]{1,0:T(8,128)(2,1)}, bf16[2,3,128,128]{3,2,1,0:T(8,128)(2,1)}, bf16[8,512,256]{2,1,0:T(8,128)(2,1)}) custom-call(s32[16,4]{1,0:T(8,128)} %copy.12.table, bf16[1024,512]{1,0:T(8,128)(2,1)} %q.5, bf16[1024,512]{1,0:T(8,128)(2,1)} %k.5, bf16[1024,512]{1,0:T(8,128)(2,1)} %v.5, bf16[1024,1024]{1,0:T(8,128)(2,1)} %og.1, ...), custom_call_target="tpu_custom_call" | custom-call | tf_op jit(solution)/shard_map/gather/pallas_call | solution.py:493
  63.0 16.3 %sparse.1 = (bf16[1024,128]{1,0:T(8,128)(2,1)}, bf16[1024,128]{1,0:T(8,128)(2,1)}, f32[1024,128]{1,0:T(8,128)}, f32[1024,128]{1,0:T(8,128)}, bf16[8,512,256]{2,1,0:T(8,128)(2,1)}) custom-call(s32[16,4]{1,0:T(8,128)} %copy.12.table, s32[1]{0:T(128)} %bitcast.place, bf16[1024,512]{1,0:T(8,128)(2,1)} %q.5, bf16[1024,512]{1,0:T(8,128)(2,1)} %k.5, ...), custom_call_target="tpu_custom_call" | custom-call | tf_op jit(solution)/shard_map/sparse/pallas_call | solution.py:538
  79.3 76.2 %scatter.1 = (bf16[1024,1024]{1,0:T(8,128)(2,1)}, bf16[1024,512]{1,0:T(8,128)(2,1)}, bf16[1024,512]{1,0:T(8,128)(2,1)}, bf16[1024,512]{1,0:T(8,128)(2,1)}) custom-call(s32[16,4]{1,0:T(8,128)} %copy.12.table, bf16[1024,512]{1,0:T(8,128)(2,1)} %q.5, bf16[1024,512]{1,0:T(8,128)(2,1)} %k.5, bf16[1024,512]{1,0:T(8,128)(2,1)} %v.5, ...), custom_call_target="tpu_custom_call" | custom-call | tf_op jit(solution)/shard_map/scatter/pallas_call | solution.py:563
  155.5 0.0 copy-start.2
  155.5 3.2 %copy.17 = bf16[1024,1024]{1,0:T(8,128)(2,1)} copy(bf16[1024,1024]{1,0:T(8,128)(2,1)} %get-tuple-element.26) | data formatting | bytes 4194304
  158.6 0.0 copy-done.2
  158.6 0.0 copy-start.1
  158.6 0.0 copy-start
  158.6 1.0 copy.18
  159.6 0.6 copy-done.1
  160.2 1.0 copy.19
  161.2 0.0 copy-done
  161.2 1.0 copy.20
Async XLA Ops:
  155.5 3.2 %copy-start.2 = (bf16[1024,512]{1,0:T(8,128)(2,1)S(1)}, bf16[1024,512]{1,0:T(8,128)(2,1)}, u32[]{:S(2)}) copy-start(bf16[1024,512]{1,0:T(8,128)(2,1)} %get-tuple-element.27) | copy-start | bytes 3145732
  158.6 1.6 copy-start.1
  158.6 2.6 %copy-start = (bf16[1024,512]{1,0:T(8,128)(2,1)S(1)}, bf16[1024,512]{1,0:T(8,128)(2,1)}, u32[]{:S(2)}) copy-start(bf16[1024,512]{1,0:T(8,128)(2,1)} %get-tuple-element.29) | copy-start | bytes 3145732

commit v3 on v2

--- a/solution.py
+++ b/solution.py
@@ -393,17 +393,22 @@
         to_far[part(c)] = bf16(product(c, far))
         far_copy(c).start()
 
-    loop(0, chunks, far_step)
-
     def par_step(c):
         mine = product(c, par)
         far_copy(c).wait_recv()
         to_par[part(c)] = bf16(mine + from_far[part(c)].astype(jnp.float32))
         par_copy(c).start()
 
-    loop(0, chunks, par_step)
-
+    def both_step(c):
+        far_step(c + 1)
+        par_step(c)
+
+    far_step(0)
+    both_step(0)
     scan.advance(0)
+    loop(1, chunks - 1, both_step)
+    par_step(chunks - 1)
+    scan.advance(1)
 
     def sib_step(c):
         to_sib[part(c)] = bf16(product(c, sib))
@@ -415,7 +420,6 @@
         own[part(c)] = product(c, h)
 
     loop(0, chunks, own_step)
-    scan.advance(1)
 
     for b in range(nblocks):
         scale = block_scale(me, rows, b)

time: 162 us -> 166 us (1.025)
  Pallas kernels: 153 us -> 157 us
    pallas_call x1, Pallas kernels: 76.2 us -> 79.7 us  [local(): pl.pallas_call(functools.partial(scatter_kernel, n_ctx), name='scatter',...]
where the time goes in v3:
time: 166 us
  Pallas kernels  157 us (95%)
  local copies, waits for them, and re-layouts  8.07 us (5%)
    pallas_call x1, Pallas kernels, local(): pl.pallas_call(functools.partial(scatter_kernel, n_ctx), name='scatter',...  79.7 us
    pallas_call x1, Pallas kernels, local(): pl.pallas_call(functools.partial(gather_kernel, n_ctx), name='gather', ou...  61 us
    pallas_call x1, Pallas kernels, local(): pl.pallas_call(sparse_kernel, name='sparse', out_shape=(jax.ShapeDtypeStr...  16.3 us
    unnamed x11, local copies, waits for them, and re-layouts  8.07 us

profile of v3, /device:TPU:8, one launch (start us, length us, event | category | flops | bytes accessed | tf_op | source)
XLA Modules:
  0.0 165.7 jit_solution(7695321544607585466)
XLA Ops:
  0.6 1.4 copy.12.table
  2.0 61.0 %gather.1 = (bf16[1024,512]{1,0:T(8,128)(2,1)}, bf16[1024,384]{1,0:T(8,128)(2,1)}, bf16[2,3,128,128]{3,2,1,0:T(8,128)(2,1)}, bf16[8,512,256]{2,1,0:T(8,128)(2,1)}) custom-call(s32[16,4]{1,0:T(8,128)} %copy.12.table, bf16[1024,512]{1,0:T(8,128)(2,1)} %q.5, bf16[1024,512]{1,0:T(8,128)(2,1)} %k.5, bf16[1024,512]{1,0:T(8,128)(2,1)} %v.5, bf16[1024,1024]{1,0:T(8,128)(2,1)} %og.1, ...), custom_call_target="tpu_custom_call" | custom-call | tf_op jit(solution)/shard_map/gather/pallas_call | solution.py:497
  63.0 16.3 %sparse.1 = (bf16[1024,128]{1,0:T(8,128)(2,1)}, bf16[1024,128]{1,0:T(8,128)(2,1)}, f32[1024,128]{1,0:T(8,128)}, f32[1024,128]{1,0:T(8,128)}, bf16[8,512,256]{2,1,0:T(8,128)(2,1)}) custom-call(s32[16,4]{1,0:T(8,128)} %copy.12.table, s32[1]{0:T(128)} %bitcast.place, bf16[1024,512]{1,0:T(8,128)(2,1)} %q.5, bf16[1024,512]{1,0:T(8,128)(2,1)} %k.5, ...), custom_call_target="tpu_custom_call" | custom-call | tf_op jit(solution)/shard_map/sparse/pallas_call | solution.py:542
  79.3 79.7 %scatter.1 = (bf16[1024,1024]{1,0:T(8,128)(2,1)}, bf16[1024,512]{1,0:T(8,128)(2,1)}, bf16[1024,512]{1,0:T(8,128)(2,1)}, bf16[1024,512]{1,0:T(8,128)(2,1)}) custom-call(s32[16,4]{1,0:T(8,128)} %copy.12.table, bf16[1024,512]{1,0:T(8,128)(2,1)} %q.5, bf16[1024,512]{1,0:T(8,128)(2,1)} %k.5, bf16[1024,512]{1,0:T(8,128)(2,1)} %v.5, ...), custom_call_target="tpu_custom_call" | custom-call | tf_op jit(solution)/shard_map/scatter/pallas_call | solution.py:567
  159.0 0.0 copy-start.2
  159.0 3.2 %copy.17 = bf16[1024,1024]{1,0:T(8,128)(2,1)} copy(bf16[1024,1024]{1,0:T(8,128)(2,1)} %get-tuple-element.26) | data formatting | bytes 4194304
  162.2 0.0 copy-done.2
  162.2 0.0 copy-start.1
  162.2 0.0 copy-start
  162.2 1.0 copy.18
  163.1 0.6 copy-done.1
  163.8 1.0 copy.19
  164.7 0.0 copy-done
  164.7 1.0 copy.20
Async XLA Ops:
  159.0 3.2 %copy-start.2 = (bf16[1024,512]{1,0:T(8,128)(2,1)S(1)}, bf16[1024,512]{1,0:T(8,128)(2,1)}, u32[]{:S(2)}) copy-start(bf16[1024,512]{1,0:T(8,128)(2,1)} %get-tuple-element.27) | copy-start | bytes 3145732
  162.2 1.6 copy-start.1
  162.2 2.6 %copy-start = (bf16[1024,512]{1,0:T(8,128)(2,1)S(1)}, bf16[1024,512]{1,0:T(8,128)(2,1)}, u32[]{:S(2)}) copy-start(bf16[1024,512]{1,0:T(8,128)(2,1)} %get-tuple-element.29) | copy-start | bytes 3145732
